TPU v7x, 32 devices: a whole 2x2x4 slice. The times are simulated.
32 devices in a mesh: groups: 2 (over y), row: 4 (over z), col: 2 (over x), rep: 2 (over core).
Axes of the slice: x: 2, y: 2, z: 4, core: 2. Of those that a mesh axis runs over, the one named last changes fastest.
Arguments:
- left_blocks: bfloat16 [8, 4, 12, 128, 128], P(('groups', 'row'), ('col', 'rep')), parts along dimension 0, may hold values from -4 to 4
- left_coords: int32 [8, 4, 2, 12], P(('groups', 'row'), ('col', 'rep')), parts along dimension 0, may hold values from -1 to 27, as said below
- right_blocks: bfloat16 [8, 4, 12, 128, 128], P(('groups', 'row'), ('col', 'rep')), parts along dimension 0, may hold values from -4 to 4
- right_coords: int32 [8, 4, 2, 12], P(('groups', 'row'), ('col', 'rep')), parts along dimension 0, may hold values from -1 to 27, as said below
Outputs:
- product: bfloat16 [8192, 4096], P(('groups', 'row'), ('col', 'rep')), parts along dimension 0
There are 2 independent parts, one for each index of `groups`. A program takes and returns all parts, laid end to end along the dimension named above; each array names one. Nothing has to cross between parts.
Inputs may be any that keep to these rules, and one draw needn't show every extreme that they name: `left_coords`: in every tile the live slots come first and hold distinct positions; slots after them have both coordinates -1. Every tile holds at least one live slot and at most 12, and some tile holds exactly 12. `right_coords`: in every tile the live slots come first and hold distinct positions; slots after them have both coordinates -1. Every tile holds at least two live slots and at most 12, some tile exactly 12; no block row of a tile holds more than 2 live slots, and in every tile some block row holds exactly 2.
All inputs are finite; a program needn't handle non-finite values.
Results may differ from a plain program's by a relative error of at most 0.001.
Values may be sent and summed in bfloat16 or wider, within the bound.
No kernel may reach another device: no remote copies, remote signals or barrier semaphores. Data moves between devices by JAX's collectives and lax.ppermute only.
A program may use at most 64 MiB of HBM per device.

v0:
```python
import functools

import jax
import jax.numpy as jnp
from jax import lax
from jax.experimental import pallas as pl
from jax.experimental.pallas import tpu as pltpu
from jax.sharding import PartitionSpec as P

BS = 128
RB = 8
KB = 28
TAIL = 16
CR = ("col", "rep")
ANY = pl.BlockSpec(memory_space=pl.ANY)
HBM = pl.BlockSpec(memory_space=pltpu.HBM)
VMEM = pl.BlockSpec(memory_space=pltpu.VMEM)
SMEM = pl.BlockSpec(memory_space=pltpu.SMEM)


def kept(memory, *arrays):
    return [pltpu.with_memory_space_constraint(array, memory) for array in arrays]


def pack_kernel(right, right_pos, left, left_pos, right_out, left_out, pos, sems):
    rows, slots = right.shape[0], right_pos.shape[1]
    copies = [
        pltpu.make_async_copy(right, right_out.at[pl.ds(0, rows)], sems.at[0]),
        pltpu.make_async_copy(left, left_out.at[pl.ds(0, rows)], sems.at[1]),
        pltpu.make_async_copy(right_pos, pos.at[0], sems.at[2]),
        pltpu.make_async_copy(left_pos, pos.at[1], sems.at[3]),
    ]
    for copy in copies:
        copy.start()
    for i, packed in enumerate((right_out, left_out)):
        copies[2 + i].wait()
        tail = jnp.pad(pos[i].astype(jnp.float32), ((0, TAIL - 2), (0, BS - slots)))
        packed[pl.ds(rows, TAIL), :] = tail.astype(jnp.bfloat16)
    for copy in copies[:2]:
        copy.wait()


def pack(right, right_pos, left, left_pos):
    packed = pltpu.VMEM((right.shape[0] + TAIL, BS), jnp.bfloat16)
    return pl.pallas_call(
        pack_kernel,
        out_shape=(packed, packed),
        in_specs=[HBM] * 4,
        out_specs=(VMEM, VMEM),
        scratch_shapes=[
            pltpu.VMEM((2, *right_pos.shape), jnp.int32),
            pltpu.SemaphoreType.DMA((4,)),
        ],
        compiler_params=pltpu.CompilerParams(vmem_limit_bytes=4 * 2**20),
    )(*kept(pltpu.HBM, right, right_pos, left, left_pos))


def block(ref, i):
    return ref[pl.ds(pl.multiple_of(i * BS, BS), BS), :]


def read_tail(ref, rows, whole, i):
    whole[pl.ds(8 * i, 8), :] = ref[pl.ds(rows, TAIL), :][:8].astype(jnp.float32).astype(jnp.int32)


def find_pairs(lc, lp, rc, rp, slots, tab, pairs, count):
    for u in range(slots):
        at = rc[rp, u] + 1
        tab[at] = tab[at] * 32 + (u + 1)
    tab[0] = 0
    for s in range(slots):
        met = tab[lc[lp + 1, s] + 1]
        for which in (met & 31, met >> 5):
            u = jnp.maximum(which - 1, 0)
            place = jnp.maximum(lc[lp, s] * RB + rc[rp + 1, u], 0)
            pairs[count] = ((lp // 8 * slots + s) * slots + u) * 64 + place
            count = count + jnp.minimum(which, 1)
    for u in range(slots):
        tab[rc[rp, u] + 1] = 0
    return count


def add_pairs(pairs, start, end, lall, right, slots, acc, seen, touched, sent):
    def multiply(p, sent):
        pair = pairs[p]
        place = pair & 63
        slot = pair >> 6
        acc[pl.ds(pl.multiple_of(place * BS, BS), BS), :] += jnp.dot(
            block(lall, slot // slots), block(right, slot % slots), preferred_element_type=jnp.float32
        )
        touched[sent] = place
        first = 1 - seen[place]
        seen[place] = 1
        return sent + first

    return lax.fori_loop(start, end, multiply, sent)


def send_blocks(touched, sent, acc, stage, out, sem):
    def block_out(i, place):
        at = (
            pl.ds(pl.multiple_of((place >> 3) * BS, BS), BS),
            pl.ds(pl.multiple_of((place & 7) * BS, BS), BS),
        )
        return pltpu.make_async_copy(stage.at[i], out.at[at], sem)

    def send(i, carry):
        stage[i] = block(acc, touched[i]).astype(jnp.bfloat16)
        block_out(i, touched[i]).start()
        return carry

    def settle(i, carry):
        block_out(0, 0).wait()
        return carry

    lax.fori_loop(0, sent, send, 0)
    lax.fori_loop(0, sent, settle, 0)


def clear_scalars(*refs):
    for ref in refs:
        for i in range(ref.shape[0]):
            ref[i] = 0


def early_kernel(tiles, slots, links, late, *refs):
    lefts, rights = refs[:tiles], refs[tiles:-14]
    out, acc, lall, lc = refs[-14:-10]
    ltails, stage, zeros, whole, coords, tab, pairs, seen, touched, sems = refs[-10:]
    rows = slots * BS

    zeros[...] = jnp.zeros_like(zeros)
    clears = [
        pltpu.make_async_copy(zeros, out.at[pl.ds(i * BS, BS), :], sems.at[0]) for i in range(RB)
    ]
    for clear in clears:
        clear.start()
    moves = [
        pltpu.make_async_copy(ref.at[pl.ds(0, rows)], lall.at[pl.ds(j * rows, rows)], sems.at[4])
        for j, ref in enumerate(lefts)
    ]
    tails = [
        pltpu.make_async_copy(ref.at[pl.ds(rows, TAIL)], ltails.at[pl.ds(j * TAIL, TAIL)], sems.at[5])
        for j, ref in enumerate(lefts)
    ]
    for copy in tails + moves:
        copy.start()
    acc[...] = jnp.zeros_like(acc)
    for copy in tails:
        copy.wait()
    for i in range(tiles):
        read_tail(ltails, i * TAIL, whole, i)
    for b, ref in enumerate(rights):
        read_tail(ref, rows, whole, tiles + b)
    scalars = [
        pltpu.make_async_copy(whole.at[pl.ds(0, 8 * tiles)], lc, sems.at[1]),
        pltpu.make_async_copy(whole.at[pl.ds(8 * tiles, 8 * len(rights))], coords, sems.at[2]),
    ]
    for copy in scalars:
        copy.start()
    clear_scalars(tab, seen)
    for copy in scalars + moves:
        copy.wait()
    for b in range(links.shape[0]):
        lc[2, b] = links[b]
    lc[3, 0] = late[0]

    sent = jnp.int32(0)
    for b, ref in enumerate(rights):
        count = find_pairs(lc, 8 * links[b], coords, 8 * b, slots, tab, pairs, jnp.int32(0))
        sent = add_pairs(pairs, 0, count, lall, ref, slots, acc, seen, touched, sent)
    for clear in clears:
        clear.wait()
    send_blocks(touched, sent, acc, stage, out, sems.at[3])


def late_kernel(when, slots, base, lc, lall, acc, *refs):
    rights = refs[:-11]
    out, acc_out, stage, whole, coords, tab, pairs, seen, touched, sems = refs[-10:]

    def add():
        for b, ref in enumerate(rights):
            read_tail(ref, slots * BS, whole, b)
        scalars = pltpu.make_async_copy(whole, coords, sems.at[0])
        scalars.start()
        clear_scalars(tab, seen)
        scalars.wait()
        sent = jnp.int32(0)
        for b, ref in enumerate(rights):
            count = find_pairs(lc, 8 * lc[2, base + b], coords, 8 * b, slots, tab, pairs, jnp.int32(0))
            sent = add_pairs(pairs, 0, count, lall, ref, slots, acc_out, seen, touched, sent)
        send_blocks(touched, sent, acc_out, stage, out, sems.at[1])

    if when is None:
        add()
    else:
        pl.when(lc[3, 0] == when)(add)


def plan_kernel(when, slots, at, lc, tail, pairs, touched, counts, whole, coords, tab, seen, sems):
    counts[0] = 0
    counts[1] = 0

    @pl.when(lc[3, 0] == when)
    def _():
        read_tail(tail, tail.shape[0] - TAIL, whole, 0)
        scalars = pltpu.make_async_copy(whole, coords, sems.at[0])
        scalars.start()
        clear_scalars(tab, seen)
        scalars.wait()
        count = find_pairs(lc, 8 * lc[2, at], coords, 0, slots, tab, pairs, jnp.int32(0))

        def mark(p, sent):
            place = pairs[p] & 63
            touched[sent] = place
            first = 1 - seen[place]
            seen[place] = 1
            return sent + first

        counts[0] = count
        counts[1] = lax.fori_loop(0, count, mark, jnp.int32(0))


def planned_kernel(slots, pairs, touched, counts, lall, acc, first, rest, out_in, out, acc_out, stage, sems):
    cut = first.shape[0] // BS

    def multiply(p, carry):
        pair = pairs[p]
        slot = pair >> 6
        u = slot % slots

        def add(ref, i):
            acc_out[pl.ds(pl.multiple_of((pair & 63) * BS, BS), BS), :] += jnp.dot(
                block(lall, slot // slots), block(ref, i), preferred_element_type=jnp.float32
            )

        pl.when(u < cut)(lambda: add(first, u))
        pl.when(u >= cut)(lambda: add(rest, u - cut))
        return carry

    lax.fori_loop(0, counts[0], multiply, 0)
    send_blocks(touched, counts[1], acc_out, stage, out, sems.at[0])


def multiply_tiles(links, late, lefts, early, later, planned=None):
    tiles = len(lefts)
    slots = lefts[0].shape[0] // BS
    rows = slots * BS
    product = pltpu.HBM((RB * BS, RB * BS), jnp.bfloat16)
    sums = pltpu.VMEM((RB * RB * BS, BS), jnp.float32)
    scalars = lambda size: pltpu.SMEM((size,), jnp.int32)
    lists = [scalars(KB + 1), scalars(2 * slots * tiles + 8), scalars(RB * RB), scalars(RB * RB + 8)]
    stage = pltpu.VMEM((RB * RB, BS, BS), jnp.bfloat16)
    params = pltpu.CompilerParams(vmem_limit_bytes=8 * 2**20)
    out, acc, lall, lc = pl.pallas_call(
        functools.partial(early_kernel, tiles, slots),
        out_shape=(
            product,
            sums,
            pltpu.VMEM((tiles * rows, BS), jnp.bfloat16),
            pltpu.SMEM((8 * tiles, BS), jnp.int32),
        ),
        in_specs=[SMEM] * 2 + [ANY] * tiles + [VMEM] * len(early),
        out_specs=(HBM, VMEM, VMEM, SMEM),
        scratch_shapes=[
            pltpu.VMEM((tiles * TAIL, BS), jnp.bfloat16),
            stage,
            pltpu.VMEM((BS, RB * BS), jnp.bfloat16),
            pltpu.VMEM((8 * (tiles + len(early)), BS), jnp.int32),
            pltpu.SMEM((8 * len(early), BS), jnp.int32),
            *lists,
            pltpu.SemaphoreType.DMA((6,)),
        ],
        compiler_params=params,
    )(links, late, lefts[0], *kept(pltpu.HBM, *lefts[1:]), *kept(pltpu.VMEM, *early))
    for when, base, tiles_here in later:
        out, acc = pl.pallas_call(
            functools.partial(late_kernel, when, slots, base),
            out_shape=(product, sums),
            in_specs=[SMEM] + [VMEM] * (2 + len(tiles_here)) + [HBM],
            out_specs=(HBM, VMEM),
            scratch_shapes=[
                stage,
                pltpu.VMEM((8 * len(tiles_here), BS), jnp.int32),
                pltpu.SMEM((8 * len(tiles_here), BS), jnp.int32),
                *lists,
                pltpu.SemaphoreType.DMA((2,)),
            ],
            input_output_aliases={2: 1, 3 + len(tiles_here): 0},
            compiler_params=params,
        )(*kept(pltpu.SMEM, lc), *kept(pltpu.VMEM, lall, acc, *tiles_here), *kept(pltpu.HBM, out))
    if planned is None:
        return out
    when, at, first, rest = planned
    short = scalars(2 * slots + 8)
    plan = pl.pallas_call(
        functools.partial(plan_kernel, when, slots, at),
        out_shape=(short, short, scalars(2)),
        in_specs=[SMEM, VMEM],
        out_specs=(SMEM, SMEM, SMEM),
        scratch_shapes=[
            pltpu.VMEM((8, BS), jnp.int32),
            pltpu.SMEM((8, BS), jnp.int32),
            scalars(KB + 1),
            scalars(RB * RB),
            pltpu.SemaphoreType.DMA((1,)),
        ],
        compiler_params=params,
    )(*kept(pltpu.SMEM, lc), *kept(pltpu.VMEM, rest))
    return pl.pallas_call(
        functools.partial(planned_kernel, slots),
        out_shape=(product, sums),
        in_specs=[SMEM] * 3 + [VMEM] * 4 + [HBM],
        out_specs=(HBM, VMEM),
        scratch_shapes=[stage, pltpu.SemaphoreType.DMA((1,))],
        input_output_aliases={4: 1, 7: 0},
        compiler_params=params,
    )(*kept(pltpu.SMEM, *plan), *kept(pltpu.VMEM, lall, acc, first, rest), *kept(pltpu.HBM, out))[0]


def split_kernel(tile, first, rest):
    cut = first.shape[0]
    first[...] = tile[pl.ds(0, cut), :]
    rest[...] = tile[pl.ds(cut, rest.shape[0]), :]


def split(tile, cut):
    return pl.pallas_call(
        split_kernel,
        out_shape=[pltpu.VMEM((n, BS), jnp.bfloat16) for n in (cut, tile.shape[0] - cut)],
        in_specs=[VMEM],
        out_specs=[VMEM, VMEM],
        compiler_params=pltpu.CompilerParams(vmem_limit_bytes=2**20),
    )(*kept(pltpu.VMEM, tile))


def shifted(block, axis, distance):
    size = lax.axis_size(axis)
    return lax.ppermute(block, axis, [((i - distance) % size, i) for i in range(size)])


def tied(block, *others):
    return lax.optimization_barrier((block, *others))[0]


def any_grid(right, left):
    rows, cols = lax.axis_size("row"), lax.axis_size(CR)
    row, col = lax.axis_index("row"), lax.axis_index(CR)
    rights = [right] + [shifted(right, "row", d) for d in range(1, rows)]
    lefts = [left] + [shifted(left, CR, d) for d in range(1, cols)]
    held = (row - jnp.arange(rows)) % rows
    links = (col - held) % cols
    late = jnp.zeros((1,), jnp.int32)
    return links.astype(jnp.int32), late, lefts, rights[:1], [(None, 1, rights[1:])]


def line_of_four(right, left):
    row, col = lax.axis_index("row"), lax.axis_index(CR)

    def along(block, route):
        return lax.ppermute(block, "row", route)

    across, swap = [(i, i ^ 2) for i in range(4)], [(i, i ^ 1) for i in range(4)]
    from_far = along(right, [(0, 2), (3, 1)])
    from_mirror = along(right, [(1, 2), (2, 1), (0, 3), (3, 0)])
    from_pair = along(right, [(0, 1), (1, 0), (2, 3), (3, 2)])
    left_x = lax.ppermute(left, CR, across)
    left_c = lax.ppermute(left, CR, swap)
    left_xc = lax.ppermute(left_x, CR, swap)
    inward = [(1, 0), (2, 3)]
    first, rest = split(from_mirror, 5 * BS)
    relayed = [along(first, inward), along(rest, inward)]

    held = jnp.stack([row, 3 - row, row ^ 1, row ^ 2])
    links = held ^ col
    late = jnp.where((row == 0) | (row == 3), 1, 0).astype(jnp.int32).reshape(1)
    lefts = [left, left_c, left_x, left_xc]
    early = [right, from_mirror, from_pair]
    return links.astype(jnp.int32), late, lefts, early, [(0, 3, [from_far])], (1, 3, *relayed)


def per_device(left_blocks, left_coords, right_blocks, right_coords):
    grid = (lax.axis_size("row"), lax.axis_size("col"), lax.axis_size("rep"))
    gather = line_of_four if grid == (4, 2, 2) else any_grid
    right, left = pack(
        right_blocks.reshape(-1, BS), right_coords[0, 0], left_blocks.reshape(-1, BS), left_coords[0, 0]
    )
    return multiply_tiles(*gather(right, left))


def solution(mesh):
    return jax.shard_map(
        per_device,
        mesh=mesh,
        in_specs=(
            P(("groups", "row"), CR, None, None, None),
            P(("groups", "row"), CR, None, None),
            P(("groups", "row"), CR, None, None, None),
            P(("groups", "row"), CR, None, None),
        ),
        out_specs=P(("groups", "row"), CR),
        check_vma=False,
    )
```

profile of v0, /device:TPU:0, one launch (start us, length us, event | category | flops | bytes accessed | tf_op | source)
XLA Modules:
  0.0 34.7 jit_solution(16741919574803552827)
XLA Ops:
  0.0 1.1 %shard_map.46 = (bf16[1552,128]{1,0:T(8,128)(2,1)S(1)}, bf16[1552,128]{1,0:T(8,128)(2,1)S(1)}) custom-call(bf16[1536,128]{1,0:T(8,128)(2,1)} %bitcast.9, s32[2,12]{1,0:T(2,128)} %bitcast.11, bf16[1536,128]{1,0:T(8,128)(2,1)} %bitcast.10, s32[2,12]{1,0:T(2,128)} %bitcast.12), custom_call_target="tpu_custom_call" | custom-call | tf_op jit(solution)/shard_map/pallas_call | solution.py:45
  1.2 3.0 %collective-permute-start.1 = (bf16[1552,128]{1,0:T(8,128)(2,1)S(1)}, bf16[1552,128]{1,0:T(8,128)(2,1)S(1)}, u32[]{:S(2)}, u32[]{:S(2)}) collective-permute-start(bf16[1552,128]{1,0:T(8,128)(2,1)S(1)} %get-tuple-element.19.refs_0_), channel_id=1, source_target_pairs={{0,2},{1,3},{2,0},{3,1},{4,6},{5,7},{6,4},{7,5},{8,10},{9,11},{10,... | collective-permute-start | bytes 1191944 | tf_op jit(solution)/shard_map/ppermute | solution.py:367
  4.2 3.6 %collective-permute-start.3 = (bf16[1552,128]{1,0:T(8,128)(2,1)S(1)}, bf16[1552,128]{1,0:T(8,128)(2,1)S(1)}, u32[]{:S(2)}, u32[]{:S(2)}) collective-permute-start(bf16[1552,128]{1,0:T(8,128)(2,1)S(1)} %get-tuple-element.20.refs_4_), channel_id=1, source_target_pairs={{4,8},{8,4},{0,12},{12,0},{5,9},{9,5},{1,13},{13,1},{6,10},{10,6},... | collective-permute-start | bytes 1191944 | tf_op jit(solution)/shard_map/ppermute | solution.py:361
  7.8 0.0 collective-permute-start
  7.8 0.0 collective-permute-start.4
  7.8 5.6 %collective-permute-done.1.refs_2_ = bf16[1552,128]{1,0:T(8,128)(2,1)S(1)} collective-permute-done((bf16[1552,128]{1,0:T(8,128)(2,1)S(1)}, bf16[1552,128]{1,0:T(8,128)(2,1)S(1)}, u32[]{:S(2)}, u32[]{:S(2)}) %collective-permute-start.1) | collective-permute-done | bytes 397344 | tf_op jit(solution)/shard_map/ppermute | solution.py:367
  13.4 0.0 copy-start
  13.4 0.0 collective-permute-start.2
  13.4 4.8 %collective-permute-start.6 = (bf16[1552,128]{1,0:T(8,128)(2,1)S(1)}, bf16[1552,128]{1,0:T(8,128)(2,1)S(1)}, u32[]{:S(2)}, u32[]{:S(2)}) collective-permute-start(bf16[1552,128]{1,0:T(8,128)(2,1)S(1)} %get-tuple-element.20.refs_4_), channel_id=1, source_target_pairs={{0,8},{12,4},{1,9},{13,5},{2,10},{14,6},{3,11},{15,7},{16,24},{28,... | collective-permute-start | bytes 1191944 | tf_op jit(solution)/shard_map/ppermute | solution.py:361
  18.1 0.0 collective-permute-done.3.refs_5_.tile
  18.2 1.3 %collective-permute-start.5 = (bf16[912,128]{1,0:T(8,128)(2,1)S(1)}, bf16[912,128]{1,0:T(8,128)(2,1)S(1)}, u32[]{:S(2)}, u32[]{:S(2)}) collective-permute-start(bf16[912,128]{1,0:T(8,128)(2,1)S(1)} %get-tuple-element.22), channel_id=1, source_target_pairs={{4,0},{8,12},{5,1},{9,13},{6,2},{10,14},{7,3},{11,15},{20,16},{24,... | collective-permute-start | bytes 700424 | tf_op jit(solution)/shard_map/ppermute | solution.py:361
  19.5 0.0 collective-permute-done.refs_1_
  19.5 0.0 copy-start.1
  19.5 1.3 %collective-permute-start.7 = (bf16[640,128]{1,0:T(8,128)(2,1)S(1)}, bf16[640,128]{1,0:T(8,128)(2,1)S(1)}, u32[]{:S(2)}, u32[]{:S(2)}) collective-permute-start(bf16[640,128]{1,0:T(8,128)(2,1)S(1)} %get-tuple-element.30), channel_id=1, source_target_pairs={{4,0},{8,12},{5,1},{9,13},{6,2},{10,14},{7,3},{11,15},{20,16},{24,... | collective-permute-start | bytes 491528 | tf_op jit(solution)/shard_map/ppermute | solution.py:361
  20.8 0.0 copy-done.1
  20.8 0.1 add_xor_fusion.links
  20.9 5.0 %collective-permute-done.4.refs_6_ = bf16[1552,128]{1,0:T(8,128)(2,1)S(1)} collective-permute-done((bf16[1552,128]{1,0:T(8,128)(2,1)S(1)}, bf16[1552,128]{1,0:T(8,128)(2,1)S(1)}, u32[]{:S(2)}, u32[]{:S(2)}) %collective-permute-start.4) | collective-permute-done | bytes 397344 | tf_op jit(solution)/shard_map/ppermute | solution.py:361
  25.9 0.0 collective-permute-done.2.refs_3_
  25.9 0.0 copy-done
  25.9 5.1 %shard_map.47 = (bf16[1024,1024]{1,0:T(8,128)(2,1)}, f32[8192,128]{1,0:T(8,128)S(1)}, bf16[6144,128]{1,0:T(8,128)(2,1)S(1)}, s32[32,128]{1,0:T(8,128)S(4)}) custom-call(s32[4]{0:T(128)S(1)} %add_xor_fusion.links, s32[1]{0:T(128)} %bitcast.4.late, bf16[1552,128]{1,0:T(8,128)(2,1)S(1)} %get-tuple-element.19.refs_0_, bf16[1552,128]{1,0:T(8,128)(2,1)} %copy-done.1, ...), custom_call_target="tpu_custom_call" | custom-call | tf_op jit(solution)/shard_map/pallas_call | solution.py:255
  31.1 1.9 %collective-permute-done.5.tail.rest = bf16[912,128]{1,0:T(8,128)(2,1)S(1)} collective-permute-done((bf16[912,128]{1,0:T(8,128)(2,1)S(1)}, bf16[912,128]{1,0:T(8,128)(2,1)S(1)}, u32[]{:S(2)}, u32[]{:S(2)}) %collective-permute-start.5) | collective-permute-done | bytes 233504 | tf_op jit(solution)/shard_map/ppermute | solution.py:361
  32.9 0.9 %shard_map.49 = (s32[32]{0:T(128)S(4)}, s32[32]{0:T(128)S(4)}, s32[2]{0:T(128)S(4)}) custom-call(s32[32,128]{1,0:T(8,128)S(4)} %get-tuple-element.21.lc, bf16[912,128]{1,0:T(8,128)(2,1)S(1)} %collective-permute-done.5.tail.rest), custom_call_target="tpu_custom_call" | custom-call | tf_op jit(solution)/shard_map/pallas_call | solution.py:296
  33.8 0.0 collective-permute-done.6.refs_0_
  33.9 0.8 %collective-permute-done.7.first = bf16[640,128]{1,0:T(8,128)(2,1)S(1)} collective-permute-done((bf16[640,128]{1,0:T(8,128)(2,1)S(1)}, bf16[640,128]{1,0:T(8,128)(2,1)S(1)}, u32[]{:S(2)}, u32[]{:S(2)}) %collective-permute-start.7) | collective-permute-done | bytes 163872 | tf_op jit(solution)/shard_map/ppermute | solution.py:361
  (3 shorter events, 0.1 us)
Async XLA Ops:
  1.2 12.2 %collective-permute-start.1 = (bf16[1552,128]{1,0:T(8,128)(2,1)S(1)}, bf16[1552,128]{1,0:T(8,128)(2,1)S(1)}, u32[]{:S(2)}, u32[]{:S(2)}) collective-permute-start(bf16[1552,128]{1,0:T(8,128)(2,1)S(1)} %get-tuple-element.19.refs_0_), channel_id=1, source_target_pairs={{0,2},{1,3},{2,0},{3,1},{4,6},{5,7},{6,4},{7,5},{8,10},{9,11},{10,... | collective-permute-start | bytes 1191944 | tf_op jit(solution)/shard_map/ppermute | solution.py:367
  4.2 14.0 %collective-permute-start.3 = (bf16[1552,128]{1,0:T(8,128)(2,1)S(1)}, bf16[1552,128]{1,0:T(8,128)(2,1)S(1)}, u32[]{:S(2)}, u32[]{:S(2)}) collective-permute-start(bf16[1552,128]{1,0:T(8,128)(2,1)S(1)} %get-tuple-element.20.refs_4_), channel_id=1, source_target_pairs={{4,8},{8,4},{0,12},{12,0},{5,9},{9,5},{1,13},{13,1},{6,10},{10,6},... | collective-permute-start | bytes 1191944 | tf_op jit(solution)/shard_map/ppermute | solution.py:361
  7.8 11.7 %collective-permute-start = (bf16[1552,128]{1,0:T(8,128)(2,1)S(1)}, bf16[1552,128]{1,0:T(8,128)(2,1)S(1)}, u32[]{:S(2)}, u32[]{:S(2)}) collective-permute-start(bf16[1552,128]{1,0:T(8,128)(2,1)S(1)} %get-tuple-element.19.refs_0_), channel_id=1, source_target_pairs={{0,1},{1,0},{2,3},{3,2},{4,5},{5,4},{6,7},{7,6},{8,9},{9,8},{10,11... | collective-permute-start | bytes 1191944 | tf_op jit(solution)/shard_map/ppermute | solution.py:368
  7.8 18.2 %collective-permute-start.4 = (bf16[1552,128]{1,0:T(8,128)(2,1)S(1)}, bf16[1552,128]{1,0:T(8,128)(2,1)S(1)}, u32[]{:S(2)}, u32[]{:S(2)}) collective-permute-start(bf16[1552,128]{1,0:T(8,128)(2,1)S(1)} %get-tuple-element.20.refs_4_), channel_id=1, source_target_pairs={{0,4},{4,0},{8,12},{12,8},{1,5},{5,1},{9,13},{13,9},{2,6},{6,2},{1... | collective-permute-start | bytes 1191944 | tf_op jit(solution)/shard_map/ppermute | solution.py:361
  13.4 12.6 %copy-start = (bf16[1552,128]{1,0:T(8,128)(2,1)}, bf16[1552,128]{1,0:T(8,128)(2,1)S(1)}, u32[]{:S(2)}) copy-start(bf16[1552,128]{1,0:T(8,128)(2,1)S(1)} %collective-permute-done.1.refs_2_) | copy-start | bytes 1191940
  13.4 12.6 %collective-permute-start.2 = (bf16[1552,128]{1,0:T(8,128)(2,1)S(1)}, bf16[1552,128]{1,0:T(8,128)(2,1)}, u32[]{:S(2)}, u32[]{:S(2)}) collective-permute-start(bf16[1552,128]{1,0:T(8,128)(2,1)S(1)} %collective-permute-done.1.refs_2_), channel_id=1, source_target_pairs={{0,1},{1,0},{2,3},{3,2},{4,5},{5,4},{6,7},{7,6},{8,9},{9,8},{10,11... | collective-permute-start | bytes 1191944 | tf_op jit(solution)/shard_map/ppermute | solution.py:369
  13.4 20.4 %collective-permute-start.6 = (bf16[1552,128]{1,0:T(8,128)(2,1)S(1)}, bf16[1552,128]{1,0:T(8,128)(2,1)S(1)}, u32[]{:S(2)}, u32[]{:S(2)}) collective-permute-start(bf16[1552,128]{1,0:T(8,128)(2,1)S(1)} %get-tuple-element.20.refs_4_), channel_id=1, source_target_pairs={{0,8},{12,4},{1,9},{13,5},{2,10},{14,6},{3,11},{15,7},{16,24},{28,... | collective-permute-start | bytes 1191944 | tf_op jit(solution)/shard_map/ppermute | solution.py:361
  18.2 14.8 %collective-permute-start.5 = (bf16[912,128]{1,0:T(8,128)(2,1)S(1)}, bf16[912,128]{1,0:T(8,128)(2,1)S(1)}, u32[]{:S(2)}, u32[]{:S(2)}) collective-permute-start(bf16[912,128]{1,0:T(8,128)(2,1)S(1)} %get-tuple-element.22), channel_id=1, source_target_pairs={{4,0},{8,12},{5,1},{9,13},{6,2},{10,14},{7,3},{11,15},{20,16},{24,... | collective-permute-start | bytes 700424 | tf_op jit(solution)/shard_map/ppermute | solution.py:361
  19.5 1.3 %copy-start.1 = (bf16[1552,128]{1,0:T(8,128)(2,1)}, bf16[1552,128]{1,0:T(8,128)(2,1)S(1)}, u32[]{:S(2)}) copy-start(bf16[1552,128]{1,0:T(8,128)(2,1)S(1)} %collective-permute-done.refs_1_) | copy-start | bytes 1191940
  19.5 15.2 %collective-permute-start.7 = (bf16[640,128]{1,0:T(8,128)(2,1)S(1)}, bf16[640,128]{1,0:T(8,128)(2,1)S(1)}, u32[]{:S(2)}, u32[]{:S(2)}) collective-permute-start(bf16[640,128]{1,0:T(8,128)(2,1)S(1)} %get-tuple-element.30), channel_id=1, source_target_pairs={{4,0},{8,12},{5,1},{9,13},{6,2},{10,14},{7,3},{11,15},{20,16},{24,... | collective-permute-start | bytes 491528 | tf_op jit(solution)/shard_map/ppermute | solution.py:361
where the time goes:
time: 35.3 us; the launch traced here: 34.7 us
  starting transfers between devices  14 us (40%)
  waiting for transfers between devices  13.3 us (38%)
  Pallas kernels  7.22 us (20%)
    ppermute x5, starting transfers between devices, along(): return lax.ppermute(block, 'row', route)  10.9 us
    ppermute x5, waiting for transfers between devices, along(): return lax.ppermute(block, 'row', route)  7.72 us
    ppermute x1, waiting for transfers between devices, line_of_four(): left_x = lax.ppermute(left, CR, across)  5.59 us
    pallas_call x1, Pallas kernels, multiply_tiles(): pl.pallas_call(functools.partial(early_kernel, tiles, slots), out_shape=(...  5.14 us
    ppermute x1, starting transfers between devices, line_of_four(): left_x = lax.ppermute(left, CR, across)  3 us
    pallas_call x1, Pallas kernels, pack(): pl.pallas_call(pack_kernel, out_shape=(packed, packed), in_specs=[HBM] *...  1.15 us
    pallas_call x1, Pallas kernels, multiply_tiles(): pl.pallas_call(functools.partial(plan_kernel, when, slots, at), out_shape...  0.86 us
  transfers between devices with their start and end apart: 8, of which 4 were waited for; matrix products, arithmetic and copies ran while one was open for 0% of the time, Pallas kernels for 17%

commit v1 on v0

--- a/solution.py
+++ b/solution.py
@@ -197,49 +197,61 @@
         pl.when(lc[3, 0] == when)(add)
 
 
-def plan_kernel(when, slots, at, lc, tail, pairs, touched, counts, whole, coords, tab, seen, sems):
+def first_kernel(when, slots, at, lc, lall, acc, first, out_in, *refs):
+    out, acc_out, later, places, counts = refs[:5]
+    stage, whole, coords, tab, pairs, seen, touched, sems = refs[5:]
+    cut = first.shape[0] // BS
     counts[0] = 0
     counts[1] = 0
 
     @pl.when(lc[3, 0] == when)
     def _():
-        read_tail(tail, tail.shape[0] - TAIL, whole, 0)
+        read_tail(first, first.shape[0] - TAIL, whole, 0)
         scalars = pltpu.make_async_copy(whole, coords, sems.at[0])
         scalars.start()
         clear_scalars(tab, seen)
         scalars.wait()
         count = find_pairs(lc, 8 * lc[2, at], coords, 0, slots, tab, pairs, jnp.int32(0))
 
+        def part(p, taken):
+            here, there = taken
+            pair = pairs[p]
+            is_here = jnp.where((pair >> 6) % slots < cut, 1, 0)
+            later[there] = pair
+            pairs[here] = pair
+            return here + is_here, there + 1 - is_here
+
+        here, there = lax.fori_loop(0, count, part, (jnp.int32(0), jnp.int32(0)))
+        sent = add_pairs(pairs, 0, here, lall, first, slots, acc_out, seen, touched, jnp.int32(0))
+        send_blocks(touched, sent, acc_out, stage, out, sems.at[1])
+        clear_scalars(seen)
+
         def mark(p, sent):
-            place = pairs[p] & 63
-            touched[sent] = place
-            first = 1 - seen[place]
+            place = later[p] & 63
+            places[sent] = place
+            new = 1 - seen[place]
             seen[place] = 1
-            return sent + first
-
-        counts[0] = count
-        counts[1] = lax.fori_loop(0, count, mark, jnp.int32(0))
-
-
-def planned_kernel(slots, pairs, touched, counts, lall, acc, first, rest, out_in, out, acc_out, stage, sems):
-    cut = first.shape[0] // BS
+            return sent + new
+
+        counts[0] = there
+        counts[1] = lax.fori_loop(0, there, mark, jnp.int32(0))
+
+
+def rest_kernel(slots, pairs, places, counts, lall, acc, rest, out_in, out, acc_out, stage, sems):
+    cut = slots - rest.shape[0] // BS
 
     def multiply(p, carry):
         pair = pairs[p]
         slot = pair >> 6
-        u = slot % slots
-
-        def add(ref, i):
-            acc_out[pl.ds(pl.multiple_of((pair & 63) * BS, BS), BS), :] += jnp.dot(
-                block(lall, slot // slots), block(ref, i), preferred_element_type=jnp.float32
-            )
-
-        pl.when(u < cut)(lambda: add(first, u))
-        pl.when(u >= cut)(lambda: add(rest, u - cut))
+        acc_out[pl.ds(pl.multiple_of((pair & 63) * BS, BS), BS), :] += jnp.dot(
+            block(lall, slot // slots),
+            block(rest, slot % slots - cut),
+            preferred_element_type=jnp.float32,
+        )
         return carry
 
     lax.fori_loop(0, counts[0], multiply, 0)
-    send_blocks(touched, counts[1], acc_out, stage, out, sems.at[0])
+    send_blocks(places, counts[1], acc_out, stage, out, sems.at[0])
 
 
 def multiply_tiles(links, late, lefts, early, later, planned=None):
@@ -273,6 +285,24 @@
         ],
         compiler_params=params,
     )(links, late, lefts[0], *kept(pltpu.HBM, *lefts[1:]), *kept(pltpu.VMEM, *early))
+    if planned is not None:
+        when, at, first, rest = planned
+        short = scalars(2 * slots + 8)
+        out, acc, *plan = pl.pallas_call(
+            functools.partial(first_kernel, when, slots, at),
+            out_shape=(product, sums, short, short, scalars(2)),
+            in_specs=[SMEM] + [VMEM] * 3 + [HBM],
+            out_specs=(HBM, VMEM, SMEM, SMEM, SMEM),
+            scratch_shapes=[
+                stage,
+                pltpu.VMEM((8, BS), jnp.int32),
+                pltpu.SMEM((8, BS), jnp.int32),
+                *lists,
+                pltpu.SemaphoreType.DMA((2,)),
+            ],
+            input_output_aliases={2: 1, 4: 0},
+            compiler_params=params,
+        )(*kept(pltpu.SMEM, lc), *kept(pltpu.VMEM, lall, acc, first), *kept(pltpu.HBM, out))
     for when, base, tiles_here in later:
         out, acc = pl.pallas_call(
             functools.partial(late_kernel, when, slots, base),
@@ -291,43 +321,29 @@
         )(*kept(pltpu.SMEM, lc), *kept(pltpu.VMEM, lall, acc, *tiles_here), *kept(pltpu.HBM, out))
     if planned is None:
         return out
-    when, at, first, rest = planned
-    short = scalars(2 * slots + 8)
-    plan = pl.pallas_call(
-        functools.partial(plan_kernel, when, slots, at),
-        out_shape=(short, short, scalars(2)),
-        in_specs=[SMEM, VMEM],
-        out_specs=(SMEM, SMEM, SMEM),
-        scratch_shapes=[
-            pltpu.VMEM((8, BS), jnp.int32),
-            pltpu.SMEM((8, BS), jnp.int32),
-            scalars(KB + 1),
-            scalars(RB * RB),
-            pltpu.SemaphoreType.DMA((1,)),
-        ],
-        compiler_params=params,
-    )(*kept(pltpu.SMEM, lc), *kept(pltpu.VMEM, rest))
     return pl.pallas_call(
-        functools.partial(planned_kernel, slots),
+        functools.partial(rest_kernel, slots),
         out_shape=(product, sums),
-        in_specs=[SMEM] * 3 + [VMEM] * 4 + [HBM],
+        in_specs=[SMEM] * 3 + [VMEM] * 3 + [HBM],
         out_specs=(HBM, VMEM),
         scratch_shapes=[stage, pltpu.SemaphoreType.DMA((1,))],
-        input_output_aliases={4: 1, 7: 0},
+        input_output_aliases={4: 1, 6: 0},
         compiler_params=params,
-    )(*kept(pltpu.SMEM, *plan), *kept(pltpu.VMEM, lall, acc, first, rest), *kept(pltpu.HBM, out))[0]
+    )(*kept(pltpu.SMEM, *plan), *kept(pltpu.VMEM, lall, acc, rest), *kept(pltpu.HBM, out))[0]
 
 
 def split_kernel(tile, first, rest):
-    cut = first.shape[0]
-    first[...] = tile[pl.ds(0, cut), :]
-    rest[...] = tile[pl.ds(cut, rest.shape[0]), :]
+    cut, rows = first.shape[0] - TAIL, tile.shape[0] - TAIL
+    first[pl.ds(0, cut), :] = tile[pl.ds(0, cut), :]
+    first[pl.ds(cut, TAIL), :] = tile[pl.ds(rows, TAIL), :]
+    rest[...] = tile[pl.ds(cut, rows - cut), :]
 
 
 def split(tile, cut):
+    rows = tile.shape[0] - TAIL
     return pl.pallas_call(
         split_kernel,
-        out_shape=[pltpu.VMEM((n, BS), jnp.bfloat16) for n in (cut, tile.shape[0] - cut)],
+        out_shape=[pltpu.VMEM((n, BS), jnp.bfloat16) for n in (cut + TAIL, rows - cut)],
         in_specs=[VMEM],
         out_specs=[VMEM, VMEM],
         compiler_params=pltpu.CompilerParams(vmem_limit_bytes=2**20),
@@ -368,7 +384,7 @@
     left_c = lax.ppermute(left, CR, swap)
     left_xc = lax.ppermute(left_x, CR, swap)
     inward = [(1, 0), (2, 3)]
-    first, rest = split(from_mirror, 5 * BS)
+    first, rest = split(from_mirror, 8 * BS)
     relayed = [along(first, inward), along(rest, inward)]
 
     held = jnp.stack([row, 3 - row, row ^ 1, row ^ 2])

time: 35.3 us -> 36 us (1.020); the launches traced: 34.7 us -> 36 us
  waiting for transfers between devices: 13.3 us -> 14.1 us
  Pallas kernels: 7.22 us -> 7.67 us
    pallas_call x2, Pallas kernels: 0.87 us -> 2.63 us  [the longest x1 1.83 us: multiply_tiles(): pl.pallas_call(functools.partial(first_kernel, when, slots, at), out_shap...]
    pallas_call x1, Pallas kernels: 5.14 us -> 3.84 us  [multiply_tiles(): pl.pallas_call(functools.partial(early_kernel, tiles, slots), out_shape=(...]
    ppermute x5, waiting for transfers between devices: 7.72 us -> 8.54 us  [along(): return lax.ppermute(block, 'row', route)]
  transfers between devices with their start and end apart: 8 -> 8, of which waited for: 4 -> 3; matrix products, arithmetic and copies ran while one was open for 0% -> 0% of each run, Pallas kernels for 17% -> 16%
where the time goes in v1:
time: 36 us
  waiting for transfers between devices  14.1 us (39%)
  starting transfers between devices  14 us (39%)
  Pallas kernels  7.67 us (21%)
    ppermute x5, starting transfers between devices, along(): return lax.ppermute(block, 'row', route)  10.9 us
    ppermute x5, waiting for transfers between devices, along(): return lax.ppermute(block, 'row', route)  8.54 us
    ppermute x1, waiting for transfers between devices, line_of_four(): left_x = lax.ppermute(left, CR, across)  5.59 us
    pallas_call x1, Pallas kernels, multiply_tiles(): pl.pallas_call(functools.partial(early_kernel, tiles, slots), out_shape=(...  3.84 us
    ppermute x1, starting transfers between devices, line_of_four(): left_x = lax.ppermute(left, CR, across)  3 us
    pallas_call x1, Pallas kernels, multiply_tiles(): pl.pallas_call(functools.partial(first_kernel, when, slots, at), out_shap...  1.83 us
    pallas_call x1, Pallas kernels, pack(): pl.pallas_call(pack_kernel, out_shape=(packed, packed), in_specs=[HBM] *...  1.15 us
    pallas_call x1, Pallas kernels, multiply_tiles(): pl.pallas_call(functools.partial(rest_kernel, slots), out_shape=(product,...  0.8 us
  transfers between devices with their start and end apart: 8, of which 3 were waited for; matrix products, arithmetic and copies ran while one was open for 0% of the time, Pallas kernels for 16%

profile of v1, /device:TPU:0, one launch (start us, length us, event | category | flops | bytes accessed | tf_op | source)
XLA Modules:
  0.0 36.0 jit_solution(15475776433111336029)
XLA Ops:
  0.0 1.1 %shard_map.46 = (bf16[1552,128]{1,0:T(8,128)(2,1)S(1)}, bf16[1552,128]{1,0:T(8,128)(2,1)S(1)}) custom-call(bf16[1536,128]{1,0:T(8,128)(2,1)} %bitcast.9, s32[2,12]{1,0:T(2,128)} %bitcast.11, bf16[1536,128]{1,0:T(8,128)(2,1)} %bitcast.10, s32[2,12]{1,0:T(2,128)} %bitcast.12), custom_call_target="tpu_custom_call" | custom-call | tf_op jit(solution)/shard_map/pallas_call | solution.py:45
  1.2 3.0 %collective-permute-start.1 = (bf16[1552,128]{1,0:T(8,128)(2,1)S(1)}, bf16[1552,128]{1,0:T(8,128)(2,1)S(1)}, u32[]{:S(2)}, u32[]{:S(2)}) collective-permute-start(bf16[1552,128]{1,0:T(8,128)(2,1)S(1)} %get-tuple-element.21.refs_0_), channel_id=1, source_target_pairs={{0,2},{1,3},{2,0},{3,1},{4,6},{5,7},{6,4},{7,5},{8,10},{9,11},{10,... | collective-permute-start | bytes 1191944 | tf_op jit(solution)/shard_map/ppermute | solution.py:383
  4.2 3.6 %collective-permute-start.3 = (bf16[1552,128]{1,0:T(8,128)(2,1)S(1)}, bf16[1552,128]{1,0:T(8,128)(2,1)S(1)}, u32[]{:S(2)}, u32[]{:S(2)}) collective-permute-start(bf16[1552,128]{1,0:T(8,128)(2,1)S(1)} %get-tuple-element.22.refs_4_), channel_id=1, source_target_pairs={{4,8},{8,4},{0,12},{12,0},{5,9},{9,5},{1,13},{13,1},{6,10},{10,6},... | collective-permute-start | bytes 1191944 | tf_op jit(solution)/shard_map/ppermute | solution.py:377
  7.8 0.0 collective-permute-start
  7.8 0.0 collective-permute-start.4
  7.8 5.6 %collective-permute-done.1.refs_2_ = bf16[1552,128]{1,0:T(8,128)(2,1)S(1)} collective-permute-done((bf16[1552,128]{1,0:T(8,128)(2,1)S(1)}, bf16[1552,128]{1,0:T(8,128)(2,1)S(1)}, u32[]{:S(2)}, u32[]{:S(2)}) %collective-permute-start.1) | collective-permute-done | bytes 397344 | tf_op jit(solution)/shard_map/ppermute | solution.py:383
  13.4 0.0 collective-permute-start.2
  13.4 4.8 %collective-permute-start.6 = (bf16[1552,128]{1,0:T(8,128)(2,1)S(1)}, bf16[1552,128]{1,0:T(8,128)(2,1)S(1)}, u32[]{:S(2)}, u32[]{:S(2)}) collective-permute-start(bf16[1552,128]{1,0:T(8,128)(2,1)S(1)} %get-tuple-element.22.refs_4_), channel_id=1, source_target_pairs={{0,8},{12,4},{1,9},{13,5},{2,10},{14,6},{3,11},{15,7},{16,24},{28,... | collective-permute-start | bytes 1191944 | tf_op jit(solution)/shard_map/ppermute | solution.py:377
  18.1 0.0 collective-permute-done.3.refs_5_.tile
  18.2 1.3 %collective-permute-start.5 = (bf16[1040,128]{1,0:T(8,128)(2,1)S(1)}, bf16[1040,128]{1,0:T(8,128)(2,1)S(1)}, u32[]{:S(2)}, u32[]{:S(2)}) collective-permute-start(bf16[1040,128]{1,0:T(8,128)(2,1)S(1)} %get-tuple-element.26), channel_id=1, source_target_pairs={{4,0},{8,12},{5,1},{9,13},{6,2},{10,14},{7,3},{11,15},{20,16},{24,... | collective-permute-start | bytes 798728 | tf_op jit(solution)/shard_map/ppermute | solution.py:377
  19.5 0.0 collective-permute-done.refs_1_
  19.5 0.0 copy-start.1
  19.5 1.3 %collective-permute-start.7 = (bf16[512,128]{1,0:T(8,128)(2,1)S(1)}, bf16[512,128]{1,0:T(8,128)(2,1)S(1)}, u32[]{:S(2)}, u32[]{:S(2)}) collective-permute-start(bf16[512,128]{1,0:T(8,128)(2,1)S(1)} %get-tuple-element.34), channel_id=1, source_target_pairs={{4,0},{8,12},{5,1},{9,13},{6,2},{10,14},{7,3},{11,15},{20,16},{24,... | collective-permute-start | bytes 393224 | tf_op jit(solution)/shard_map/ppermute | solution.py:377
  20.8 0.0 copy-done.1
  20.8 0.1 add_xor_fusion.links
  20.9 5.0 %collective-permute-done.4.refs_6_ = bf16[1552,128]{1,0:T(8,128)(2,1)S(1)} collective-permute-done((bf16[1552,128]{1,0:T(8,128)(2,1)S(1)}, bf16[1552,128]{1,0:T(8,128)(2,1)S(1)}, u32[]{:S(2)}, u32[]{:S(2)}) %collective-permute-start.4) | collective-permute-done | bytes 397344 | tf_op jit(solution)/shard_map/ppermute | solution.py:377
  25.9 0.0 collective-permute-done.2.refs_3_
  25.9 0.0 copy-done
  25.9 3.8 %shard_map.47 = (bf16[1024,1024]{1,0:T(8,128)(2,1)}, f32[8192,128]{1,0:T(8,128)S(1)}, bf16[6144,128]{1,0:T(8,128)(2,1)S(1)}, s32[32,128]{1,0:T(8,128)S(4)}) custom-call(s32[4]{0:T(128)S(1)} %add_xor_fusion.links, s32[1]{0:T(128)} %bitcast.4.late, bf16[1552,128]{1,0:T(8,128)(2,1)S(1)} %get-tuple-element.21.refs_0_, bf16[1552,128]{1,0:T(8,128)(2,1)} %copy-done.1, ...), custom_call_target="tpu_custom_call" | custom-call | tf_op jit(solution)/shard_map/pallas_call | solution.py:267
  29.8 3.5 %collective-permute-done.5.first = bf16[1040,128]{1,0:T(8,128)(2,1)S(1)} collective-permute-done((bf16[1040,128]{1,0:T(8,128)(2,1)S(1)}, bf16[1040,128]{1,0:T(8,128)(2,1)S(1)}, u32[]{:S(2)}, u32[]{:S(2)}) %collective-permute-start.5) | collective-permute-done | bytes 266272 | tf_op jit(solution)/shard_map/ppermute | solution.py:377
  33.3 1.8 %shard_map.49 = (bf16[1024,1024]{1,0:T(8,128)(2,1)}, f32[8192,128]{1,0:T(8,128)S(1)}, s32[32]{0:T(128)S(4)}, s32[32]{0:T(128)S(4)}, s32[2]{0:T(128)S(4)}) custom-call(s32[32,128]{1,0:T(8,128)S(4)} %get-tuple-element.23.lc, bf16[6144,128]{1,0:T(8,128)(2,1)S(1)} %get-tuple-element.24.lall, ...), custom_call_target="tpu_custom_call", output_to_operand_aliasing={{1}: (2, {}), {0}: (4, {})} | custom-call | tf_op jit(solution)/shard_map/pallas_call | solution.py:291
  35.1 0.0 collective-permute-done.6.refs_0_
  35.2 0.0 collective-permute-done.7.rest
  35.2 0.8 %shard_map.51 = (bf16[1024,1024]{1,0:T(8,128)(2,1)}, f32[8192,128]{1,0:T(8,128)S(1)}) custom-call(s32[32]{0:T(128)S(4)} %get-tuple-element.28.pairs, s32[32]{0:T(128)S(4)} %get-tuple-element.29.places, s32[2]{0:T(128)S(4)} %get-tuple-element.30.counts, bf16[6144,128]{1,0:T(8,128)(2,1)S(1)} %get-tuple-element.24.lall, ...), custom_call_target="tpu_custom_call", output_to_operand_aliasing={{1}: (4, {}), {0}: (6, {})} | custom-call | tf_op jit(solution)/shard_map/pallas_call | solution.py:324
  (3 shorter events, 0.1 us)
Async XLA Ops:
  1.2 12.2 %collective-permute-start.1 = (bf16[1552,128]{1,0:T(8,128)(2,1)S(1)}, bf16[1552,128]{1,0:T(8,128)(2,1)S(1)}, u32[]{:S(2)}, u32[]{:S(2)}) collective-permute-start(bf16[1552,128]{1,0:T(8,128)(2,1)S(1)} %get-tuple-element.21.refs_0_), channel_id=1, source_target_pairs={{0,2},{1,3},{2,0},{3,1},{4,6},{5,7},{6,4},{7,5},{8,10},{9,11},{10,... | collective-permute-start | bytes 1191944 | tf_op jit(solution)/shard_map/ppermute | solution.py:383
  4.2 14.0 %collective-permute-start.3 = (bf16[1552,128]{1,0:T(8,128)(2,1)S(1)}, bf16[1552,128]{1,0:T(8,128)(2,1)S(1)}, u32[]{:S(2)}, u32[]{:S(2)}) collective-permute-start(bf16[1552,128]{1,0:T(8,128)(2,1)S(1)} %get-tuple-element.22.refs_4_), channel_id=1, source_target_pairs={{4,8},{8,4},{0,12},{12,0},{5,9},{9,5},{1,13},{13,1},{6,10},{10,6},... | collective-permute-start | bytes 1191944 | tf_op jit(solution)/shard_map/ppermute | solution.py:377
  7.8 11.7 %collective-permute-start = (bf16[1552,128]{1,0:T(8,128)(2,1)S(1)}, bf16[1552,128]{1,0:T(8,128)(2,1)S(1)}, u32[]{:S(2)}, u32[]{:S(2)}) collective-permute-start(bf16[1552,128]{1,0:T(8,128)(2,1)S(1)} %get-tuple-element.21.refs_0_), channel_id=1, source_target_pairs={{0,1},{1,0},{2,3},{3,2},{4,5},{5,4},{6,7},{7,6},{8,9},{9,8},{10,11... | collective-permute-start | bytes 1191944 | tf_op jit(solution)/shard_map/ppermute | solution.py:384
  7.8 18.2 %collective-permute-start.4 = (bf16[1552,128]{1,0:T(8,128)(2,1)S(1)}, bf16[1552,128]{1,0:T(8,128)(2,1)S(1)}, u32[]{:S(2)}, u32[]{:S(2)}) collective-permute-start(bf16[1552,128]{1,0:T(8,128)(2,1)S(1)} %get-tuple-element.22.refs_4_), channel_id=1, source_target_pairs={{0,4},{4,0},{8,12},{12,8},{1,5},{5,1},{9,13},{13,9},{2,6},{6,2},{1... | collective-permute-start | bytes 1191944 | tf_op jit(solution)/shard_map/ppermute | solution.py:377
  13.4 12.6 %copy-start = (bf16[1552,128]{1,0:T(8,128)(2,1)}, bf16[1552,128]{1,0:T(8,128)(2,1)S(1)}, u32[]{:S(2)}) copy-start(bf16[1552,128]{1,0:T(8,128)(2,1)S(1)} %collective-permute-done.1.refs_2_) | copy-start | bytes 1191940
  13.4 12.6 %collective-permute-start.2 = (bf16[1552,128]{1,0:T(8,128)(2,1)S(1)}, bf16[1552,128]{1,0:T(8,128)(2,1)}, u32[]{:S(2)}, u32[]{:S(2)}) collective-permute-start(bf16[1552,128]{1,0:T(8,128)(2,1)S(1)} %collective-permute-done.1.refs_2_), channel_id=1, source_target_pairs={{0,1},{1,0},{2,3},{3,2},{4,5},{5,4},{6,7},{7,6},{8,9},{9,8},{10,11... | collective-permute-start | bytes 1191944 | tf_op jit(solution)/shard_map/ppermute | solution.py:385
  13.4 21.8 %collective-permute-start.6 = (bf16[1552,128]{1,0:T(8,128)(2,1)S(1)}, bf16[1552,128]{1,0:T(8,128)(2,1)S(1)}, u32[]{:S(2)}, u32[]{:S(2)}) collective-permute-start(bf16[1552,128]{1,0:T(8,128)(2,1)S(1)} %get-tuple-element.22.refs_4_), channel_id=1, source_target_pairs={{0,8},{12,4},{1,9},{13,5},{2,10},{14,6},{3,11},{15,7},{16,24},{28,... | collective-permute-start | bytes 1191944 | tf_op jit(solution)/shard_map/ppermute | solution.py:377
  18.2 15.1 %collective-permute-start.5 = (bf16[1040,128]{1,0:T(8,128)(2,1)S(1)}, bf16[1040,128]{1,0:T(8,128)(2,1)S(1)}, u32[]{:S(2)}, u32[]{:S(2)}) collective-permute-start(bf16[1040,128]{1,0:T(8,128)(2,1)S(1)} %get-tuple-element.26), channel_id=1, source_target_pairs={{4,0},{8,12},{5,1},{9,13},{6,2},{10,14},{7,3},{11,15},{20,16},{24,... | collective-permute-start | bytes 798728 | tf_op jit(solution)/shard_map/ppermute | solution.py:377
  19.5 1.3 %copy-start.1 = (bf16[1552,128]{1,0:T(8,128)(2,1)}, bf16[1552,128]{1,0:T(8,128)(2,1)S(1)}, u32[]{:S(2)}) copy-start(bf16[1552,128]{1,0:T(8,128)(2,1)S(1)} %collective-permute-done.refs_1_) | copy-start | bytes 1191940
  19.5 15.7 %collective-permute-start.7 = (bf16[512,128]{1,0:T(8,128)(2,1)S(1)}, bf16[512,128]{1,0:T(8,128)(2,1)S(1)}, u32[]{:S(2)}, u32[]{:S(2)}) collective-permute-start(bf16[512,128]{1,0:T(8,128)(2,1)S(1)} %get-tuple-element.34), channel_id=1, source_target_pairs={{4,0},{8,12},{5,1},{9,13},{6,2},{10,14},{7,3},{11,15},{20,16},{24,... | collective-permute-start | bytes 393224 | tf_op jit(solution)/shard_map/ppermute | solution.py:377
